TPU v7x, 256 devices: a whole 4x4x8 slice. The times are simulated.
256 devices in a mesh: sym: 8 (over z_hi, core), rad: 32 (over z_lo, x, y).
Axes of the slice: x: 4, y: 4, z: 8 (z_hi: 4, z_lo: 2; z = z_hi * 2 + z_lo), core: 2. Of those that a mesh axis runs over, the one named last changes fastest.
Arguments:
- start_amplitudes: float32 [8, 768, 32, 128], P('sym', None, 'rad'), may hold values from -6 to 6
- coupling: bfloat16 [8, 3, 768, 3, 768], P('sym'), may hold values from -0.078125 to 0.078125
- block_pattern: int32 [8, 6, 3, 6], P('sym'), may hold values 0 or 1
- counts: int32 [8], P('sym'), may hold values from 256 to 768, as said below
- radial_terms: float32 [3, 512], P(None, 'rad'), may hold values from 0.5 to 2
- energy: float32 [8, 768], P('sym'), may hold values from -3 to 3
- potential: float32 [512], replicated, may hold values from -3.140625 to 3.140625
- element_matrices: float32 [2, 4, 128, 128], replicated, may hold values from -0.375 to 0.375
Outputs:
- end_amplitudes: float32 [8, 768, 32, 128], P('sym', None, 'rad')
Inputs may be any that keep to these rules, and one draw needn't show every extreme that they name: `counts`: some symmetry has exactly 768 live channels in every draw.
All inputs are finite; a program needn't handle non-finite values. No bound on the sum of `block_pattern` on one device may be relied on, other than what follows from the above.
Results may differ from a plain program's by a relative error of at most 0.0029.
Values may be sent and summed in bfloat16 or wider, within the bound.
A program may use at most 128 MiB of HBM per device.

v0:
```python
import jax
import jax.numpy as jnp
from jax import lax
from jax.experimental import pallas as pl
from jax.experimental.pallas import tpu as pltpu
from jax.sharding import PartitionSpec as P

MESH = pl.DeviceIdType.MESH
STEP = 0.8
CH = 768
COLS = 128
HALF = CH // 2
PART = 16
GROUP = 8
ORDERS = 3
TILE = 128
FINE = 256
TERMS = 6
PHASES = 3
SELF, NEAR, FAR = 0, 1, 2
F32 = jnp.float32
BF16 = jnp.bfloat16


def split(x):
    high = x.astype(BF16)
    return high, (x - high.astype(F32)).astype(BF16)


def kernel(
    counts, pattern, start, coupling, radial, energy, potential, matrices,
    out,
    raw, wt, xbuf, rin, rout, vt, vback, acc, even, odd, cosine, sine, start_v, mat_v, bhigh, blow, rad_t,
    load_sem, w_sem, in_send, in_recv, out_send, out_recv, near_send, near_recv, far_send, far_recv,
):
    s = lax.axis_index("sym")
    q = lax.axis_index("rad")
    e = q // GROUP
    g = q % GROUP
    above_near = s % 2 == 0
    near = jnp.where(above_near, s + 1, s - 1)
    far = jnp.where(above_near, s - 1, s + 1)
    has_far = jnp.logical_and(far >= 0, far < 8)
    k_near = jnp.where(above_near, 2, 0)
    k_far = jnp.where(above_near, 0, 2)

    start_load = pltpu.make_async_copy(start, start_v, load_sem.at[0])
    start_load.start()
    mat_load = pltpu.make_async_copy(matrices.at[:, e], mat_v, load_sem.at[1])
    mat_load.start()
    w_loads = [pltpu.make_async_copy(coupling.at[i], raw.at[i], w_sem.at[i]) for i in range(9)]
    for load in w_loads:
        load.start()

    def peer(d):
        return (g + d) % GROUP

    def peer_back(d):
        return (g + GROUP - d) % GROUP

    barrier = pltpu.get_barrier_semaphore()
    for d in range(1, GROUP):
        pl.semaphore_signal(barrier, inc=1, device_id=(s, e * GROUP + peer(d)), device_id_type=MESH)
    pl.semaphore_signal(barrier, inc=1, device_id=(near, q), device_id_type=MESH)

    @pl.when(has_far)
    def _():
        pl.semaphore_signal(barrier, inc=1, device_id=(far, q), device_id_type=MESH)

    def rows_of(i):
        return pl.ds(pl.multiple_of((i // 2) * 2 * PART, 2 * PART), 2 * PART)

    def lanes_of(i):
        return pl.ds(pl.multiple_of((i % 2) * HALF, HALF), HALF)

    def in_copy(phase, d):
        i = peer(d)
        return pltpu.make_async_remote_copy(
            src_ref=vt.at[phase, rows_of(i), lanes_of(i)],
            dst_ref=rin.at[phase, g],
            send_sem=in_send.at[phase, d],
            recv_sem=in_recv.at[phase, d],
            device_id=(s, e * GROUP + i),
            device_id_type=MESH,
        )

    def out_copy(phase, d):
        i = peer(d)
        return pltpu.make_async_remote_copy(
            src_ref=rout.at[phase, i],
            dst_ref=vback.at[phase, rows_of(g), lanes_of(g)],
            send_sem=out_send.at[phase, d],
            recv_sem=out_recv.at[phase, d],
            device_id=(s, e * GROUP + i),
            device_id_type=MESH,
        )

    def near_copy(t):
        return pltpu.make_async_remote_copy(
            src_ref=xbuf.at[t, SELF],
            dst_ref=xbuf.at[t, NEAR],
            send_sem=near_send.at[t],
            recv_sem=near_recv.at[t],
            device_id=(near, q),
            device_id_type=MESH,
        )

    def far_copy(t, j):
        lanes = pl.ds(j * FINE, FINE)
        return pltpu.make_async_remote_copy(
            src_ref=xbuf.at[t, SELF, :, lanes],
            dst_ref=xbuf.at[t, FAR, :, lanes],
            send_sem=far_send.at[t, j],
            recv_sem=far_recv.at[t, j],
            device_id=(far, q),
            device_id_type=MESH,
        )

    def send_in(phase):
        for d in range(1, GROUP):
            in_copy(phase, d).start()
        rin[phase, g] = vt[phase, rows_of(g), lanes_of(g)]

    def send_far(t, j):
        @pl.when(has_far)
        def _():
            far_copy(t, j).start()

    def wait_far(t, j):
        @pl.when(has_far)
        def _():
            far_copy(t, j).wait_recv()

    start_load.wait()
    lane = lax.broadcasted_iota(jnp.int32, (COLS, CH), 1)
    live = jnp.where(lane < counts[0], 1.0, 0.0).astype(F32)
    for j in range(CH // TILE):
        cols = slice(j * TILE, (j + 1) * TILE)
        vt[0, :, cols] = start_v[cols, :].T * live[:, cols]
    pl.semaphore_wait(barrier, jnp.where(has_far, GROUP + 1, GROUP))
    send_in(0)

    mat_load.wait()
    m0, m1 = mat_v[0], mat_v[1]
    for r, (x, y) in enumerate(((m0, -m1), (m1, m0))):
        for c, part in enumerate((x, y)):
            high, low = split(part)
            bhigh[r * 128 : (r + 1) * 128, c * 128 : (c + 1) * 128] = high
            blow[r * 128 : (r + 1) * 128, c * 128 : (c + 1) * 128] = low
    pot = jnp.broadcast_to(potential[pl.ds(e, 1), :], (TILE, TILE)).T
    for j in range(HALF // TILE):
        lanes = pl.ds(pl.multiple_of((g % 2) * HALF + j * TILE, TILE), TILE)
        angle = energy[:, lanes] + pot
        cosine[:, j * TILE : (j + 1) * TILE] = jnp.cos(angle)
        sine[:, j * TILE : (j + 1) * TILE] = jnp.sin(angle)
    for l in range(ORDERS):
        rad_t[l] = jnp.broadcast_to(radial[l : l + 1, :], (TILE, TILE)).T

    @pl.when(jnp.logical_not(has_far))
    def _():
        for t in range(TERMS):
            xbuf[t, FAR] = jnp.zeros((COLS, CH), BF16)

    def turn_weights(first, last):
        def body(i, _):
            l = i // 3
            k = i % 3
            pltpu.make_async_copy(coupling.at[i], raw.at[i], w_sem.at[i]).wait()
            for a in range(CH // TILE):
                for b in range(CH // TILE):
                    keep = jnp.full((TILE, TILE), pattern[a, k, b].astype(F32), F32).astype(BF16)
                    tile = raw[i, a * TILE : (a + 1) * TILE, b * TILE : (b + 1) * TILE]
                    wt[
                        k,
                        b * TILE : (b + 1) * TILE,
                        pl.ds(pl.multiple_of(l * CH + a * TILE, TILE), TILE),
                    ] = tile.T * keep
            return 0

        lax.fori_loop(first, last, body, 0)

    def element(re, im):
        xhigh, xlow = split(jnp.concatenate((re, im), axis=0))
        y = jnp.dot(bhigh[...], xhigh, preferred_element_type=F32)
        y = y + jnp.dot(bhigh[...], xlow, preferred_element_type=F32)
        y = y + jnp.dot(blow[...], xhigh, preferred_element_type=F32)
        return y[:128], y[128:]

    def turn(re, im):
        c, n = cosine[...], sine[...]
        return re * c + im * n, im * c - re * n

    def radial_phase(phase):
        for d in range(1, GROUP):
            in_copy(phase, d).wait_recv()
        block = rin[phase].reshape(GROUP, 2, PART, HALF)
        re = block[:, 0].reshape(GROUP * PART, HALF)
        im = block[:, 1].reshape(GROUP * PART, HALF)
        re, im = element(*turn(re, im))
        if phase == 1:
            re, im = element(*turn(re, im))
        rout[phase, :, :PART, :] = re.reshape(GROUP, PART, HALF)
        rout[phase, :, PART:, :] = im.reshape(GROUP, PART, HALF)
        for d in range(1, GROUP):
            out_copy(phase, d).start()
        vback[phase, rows_of(g), lanes_of(g)] = rout[phase, g]

    def wait_back(phase):
        for d in range(1, GROUP):
            out_copy(phase, d).wait_recv()

    def term(t, scale, emit):
        acc[...] = jnp.dot(xbuf[t, SELF], wt[1], preferred_element_type=F32)
        near_copy(t).wait_recv()
        acc[...] += jnp.dot(xbuf[t, NEAR], wt[k_near], preferred_element_type=F32)
        wait_far(t, 0)
        wait_far(t, 1)
        acc[...] += jnp.dot(
            xbuf[t, FAR, :, : 2 * FINE], wt[k_far, : 2 * FINE], preferred_element_type=F32
        )
        wait_far(t, 2)
        for j in range(CH // FINE):
            total = None
            for l in range(ORDERS):
                lanes = slice(l * CH + j * FINE, l * CH + (j + 1) * FINE)
                y = acc[:, lanes] + jnp.dot(
                    xbuf[t, FAR, :, 2 * FINE :],
                    wt[k_far, 2 * FINE :, lanes],
                    preferred_element_type=F32,
                )
                factor = jnp.concatenate((rad_t[l], rad_t[l]), axis=1)
                total = y * factor if total is None else total + y * factor
            lane = lax.broadcasted_iota(jnp.int32, (COLS, FINE), 1) + j * FINE
            emit(j, jnp.where(lane < counts[0], total * scale, 0.0))

    def coupling_step(step):
        phase = step
        base = 3 * step
        xbuf[base, SELF] = vback[phase].astype(BF16)
        for j in range(3):
            send_far(base, j)
        near_copy(base).start()

        def first(j, u):
            lanes = slice(j * FINE, (j + 1) * FINE)
            odd[:, lanes] = u
            xbuf[base + 1, SELF, :, lanes] = u.astype(BF16)
            send_far(base + 1, j)

        def second(j, u):
            lanes = slice(j * FINE, (j + 1) * FINE)
            even[:, lanes] = vback[phase, :, lanes] - u
            xbuf[base + 2, SELF, :, lanes] = u.astype(BF16)
            send_far(base + 2, j)

        def third(j, u):
            lanes = slice(j * FINE, (j + 1) * FINE)
            o = odd[:, lanes] - u
            ev = even[:, lanes]
            for n in range(COLS // (2 * PART)):
                a, b, c = n * 2 * PART, n * 2 * PART + PART, (n + 1) * 2 * PART
                vt[phase + 1, a:b, lanes] = ev[a:b] + o[b:c]
                vt[phase + 1, b:c, lanes] = ev[b:c] - o[a:b]

        term(base, STEP, first)
        near_copy(base + 1).start()
        term(base + 1, STEP / 2.0, second)
        near_copy(base + 2).start()
        term(base + 2, STEP / 3.0, third)

    turn_weights(0, 5)
    radial_phase(0)
    turn_weights(5, 9)
    wait_back(0)
    coupling_step(0)
    send_in(1)
    radial_phase(1)
    wait_back(1)
    coupling_step(1)
    send_in(2)
    radial_phase(2)
    wait_back(2)
    for j in range(CH // TILE):
        cols = slice(j * TILE, (j + 1) * TILE)
        out[cols, :] = vback[2, :, cols].T

    for phase in range(PHASES):
        for d in range(1, GROUP):
            in_copy(phase, d).wait_send()
            out_copy(phase, d).wait_send()
    for t in range(TERMS):
        near_copy(t).wait_send()

        @pl.when(has_far)
        def _():
            for j in range(3):
                far_copy(t, j).wait_send()


def shards(
    start_amplitudes, coupling, block_pattern, counts, radial_terms, energy, potential, element_matrices
):
    start = start_amplitudes.reshape(CH, COLS)
    weights = coupling[0].transpose(0, 2, 1, 3).reshape(9, CH, CH)
    radial = jnp.tile(radial_terms, (1, COLS // PART))
    vmem = pl.BlockSpec(memory_space=pltpu.VMEM)
    smem = pl.BlockSpec(memory_space=pltpu.SMEM)
    anywhere = pl.BlockSpec(memory_space=pl.ANY)
    dma = pltpu.SemaphoreType.DMA
    out = pl.pallas_call(
        kernel,
        out_shape=jax.ShapeDtypeStruct((CH, COLS), F32),
        in_specs=[smem, smem, anywhere, anywhere, vmem, vmem, vmem, anywhere],
        out_specs=vmem,
        scratch_shapes=[
            pltpu.VMEM((9, CH, CH), BF16),
            pltpu.VMEM((3, CH, ORDERS * CH), BF16),
            pltpu.VMEM((TERMS, 3, COLS, CH), BF16),
            pltpu.VMEM((PHASES, GROUP, 2 * PART, HALF), F32),
            pltpu.VMEM((PHASES, GROUP, 2 * PART, HALF), F32),
            pltpu.VMEM((PHASES, COLS, CH), F32),
            pltpu.VMEM((PHASES, COLS, CH), F32),
            pltpu.VMEM((COLS, ORDERS * CH), F32),
            pltpu.VMEM((COLS, CH), F32),
            pltpu.VMEM((COLS, CH), F32),
            pltpu.VMEM((TILE, HALF), F32),
            pltpu.VMEM((TILE, HALF), F32),
            pltpu.VMEM((CH, COLS), F32),
            pltpu.VMEM((2, TILE, TILE), F32),
            pltpu.VMEM((2 * TILE, 2 * TILE), BF16),
            pltpu.VMEM((2 * TILE, 2 * TILE), BF16),
            pltpu.VMEM((ORDERS, TILE, TILE), F32),
            dma((2,)),
            dma((9,)),
            dma((PHASES, GROUP)),
            dma((PHASES, GROUP)),
            dma((PHASES, GROUP)),
            dma((PHASES, GROUP)),
            dma((TERMS,)),
            dma((TERMS,)),
            dma((TERMS, 3)),
            dma((TERMS, 3)),
        ],
        compiler_params=pltpu.CompilerParams(
            collective_id=0, has_side_effects=True, vmem_limit_bytes=52 * 2**20
        ),
    )(
        counts,
        block_pattern[0],
        start,
        weights,
        radial,
        energy,
        potential.reshape(4, TILE),
        element_matrices,
    )
    return out.reshape(1, CH, 1, COLS)


def solution(mesh):
    return jax.shard_map(
        shards,
        mesh=mesh,
        in_specs=(
            P("sym", None, "rad", None),
            P("sym", None, None, None, None),
            P("sym", None, None, None),
            P("sym"),
            P(None, "rad"),
            P("sym", None),
            P(),
            P(),
        ),
        out_specs=P("sym", None, "rad", None),
        check_vma=False,
    )
```

profile of v0, /device:TPU:1, one launch (start us, length us, event | category | flops | bytes accessed | tf_op | source)
XLA Modules:
  0.0 95.2 jit_solution(4393480415045521074)
XLA Ops:
  0.7 0.7 copy.13
  1.4 0.7 tile.4
  2.0 0.1 tile.10.radial
  2.1 0.0 copy-start
  2.1 1.0 %copy-done = f32[2,4,128,128]{3,2,1,0:T(8,128)S(1)} copy-done((f32[2,4,128,128]{3,2,1,0:T(8,128)S(1)}, f32[2,4,128,128]{3,2,1,0:T(8,128)}, u32[]{:S(2)}) %copy-start) | copy-done | bytes 524312
  3.2 0.0 copy-start.1
  3.2 1.0 %copy-done.1 = f32[1,768,1,128]{3,2,1,0:T(1,128)S(1)} copy-done((f32[1,768,1,128]{3,2,1,0:T(1,128)S(1)}, f32[1,768,1,128]{3,2,1,0:T(1,128)}, u32[]{:S(2)}) %copy-start.1) | copy-done | bytes 393240
  4.2 0.0 copy-start.2
  4.2 0.7 copy-done.2
  4.9 0.0 copy-start.3
  4.9 0.7 copy-done.3
  5.5 88.9 %shard_map.82 = f32[768,128]{1,0:T(8,128)S(1)} custom-call(s32[1]{0:T(128)S(6)} %copy.15.counts, s32[6,3,6]{2,1,0:T(4,128)S(1)} %copy.10.pattern, f32[768,128]{1,0:T(8,128)S(1)} %bitcast.14, bf16[9,768,768]{2,1,0:T(8,128)(2,1)} %bitcast.16, f32[3,128]{1,0:T(4,128)S(1)} %tile.10.radial, f32[1,768]{1,0:T(1,128)S(1)} %copy-done.2, f32[4,128]{1,0:T(4,128)S(1)} %bitcast.15, ...), custom_call_target="tpu_custom_call" | custom-call | tf_op jit(solution)/shard_map/pallas_call | solution.py:310
  94.5 0.7 copy.16
  (1 shorter events, 0.0 us)
Async XLA Ops:
  2.1 1.0 %copy-start = (f32[2,4,128,128]{3,2,1,0:T(8,128)S(1)}, f32[2,4,128,128]{3,2,1,0:T(8,128)}, u32[]{:S(2)}) copy-start(f32[2,4,128,128]{3,2,1,0:T(8,128)} %matrices.1) | copy-start | bytes 1572868
  3.2 1.0 %copy-start.1 = (f32[1,768,1,128]{3,2,1,0:T(1,128)S(1)}, f32[1,768,1,128]{3,2,1,0:T(1,128)}, u32[]{:S(2)}) copy-start(f32[1,768,1,128]{3,2,1,0:T(1,128)} %param.8) | copy-start | bytes 1179652
  4.2 0.7 copy-start.2
  4.9 0.7 copy-start.3
where the time goes:
time: 95.5 us; the launch traced here: 95.2 us
  Pallas kernels  88.9 us (93%)
  local copies, waits for them, and re-layouts  5.63 us (6%)
    pallas_call x1, Pallas kernels, shards(): pl.pallas_call(kernel, out_shape=jax.ShapeDtypeStruct((CH, COLS), F32), i...  88.9 us
    unnamed x10, local copies, waits for them, and re-layouts  4.85 us

commit v1 on v0

--- a/solution.py
+++ b/solution.py
@@ -1,3 +1,5 @@
+import math
+
 import jax
 import jax.numpy as jnp
 from jax import lax
@@ -18,6 +20,9 @@
 TERMS = 6
 PHASES = 3
 SELF, NEAR, FAR = 0, 1, 2
+BLOCK = 7
+LEVELS = 64.0
+FULL = 32760.0
 F32 = jnp.float32
 BF16 = jnp.bfloat16
 
@@ -27,11 +32,38 @@
     return high, (x - high.astype(F32)).astype(BF16)
 
 
+def pack(re, im, ref):
+    rows = lax.broadcasted_iota(jnp.int32, (PART, TILE), 0)
+    scales = jnp.zeros((PART, TILE), F32)
+    for c in range(HALF // TILE):
+        lanes = slice(c * TILE, (c + 1) * TILE)
+        a, b = re[:, lanes], im[:, lanes]
+        top = jnp.max(jnp.maximum(jnp.abs(a), jnp.abs(b)), axis=0, keepdims=True)
+        level = jnp.ceil(jnp.log(jnp.maximum(top, 1e-36)) * (LEVELS / math.log(2.0)))
+        factor = jnp.exp2(level * (-1.0 / LEVELS))
+        ref[c] = jnp.round(a * factor * FULL).astype(jnp.int32).astype(jnp.int16)
+        ref[3 + c] = jnp.round(b * factor * FULL).astype(jnp.int32).astype(jnp.int16)
+        scales = jnp.where(rows == c, level, scales)
+    ref[6] = scales.astype(jnp.int32).astype(jnp.int16)
+
+
+def unpack(ref):
+    level = ref[6].astype(jnp.int32).astype(F32)
+    factor = jnp.exp2(level * (1.0 / LEVELS)) * (1.0 / FULL)
+    parts = []
+    for first in (0, 3):
+        tiles = [
+            ref[first + c].astype(jnp.int32).astype(F32) * factor[c : c + 1] for c in range(HALF // TILE)
+        ]
+        parts.append(jnp.concatenate(tiles, axis=1))
+    return parts
+
+
 def kernel(
-    counts, pattern, start, coupling, radial, energy, potential, matrices,
+    counts, pattern_h, start, coupling, radial_h, energy_h, potential_h, matrices,
     out,
-    raw, wt, xbuf, rin, rout, vt, vback, acc, even, odd, cosine, sine, start_v, mat_v, bhigh, blow, rad_t,
-    load_sem, w_sem, in_send, in_recv, out_send, out_recv, near_send, near_recv, far_send, far_recv,
+    raw, wt, xbuf, qin, rin, qout, rback, v, acc, even, odd, cosine, sine, start_v, mat_v, bhigh, blow, rad_t,
+    pattern, radial, energy, potential, load_sem, w_sem, in_send, in_recv, out_send, out_recv, near_send, near_recv, far_send, far_recv,
 ):
     s = lax.axis_index("sym")
     q = lax.axis_index("rad")
@@ -48,6 +80,14 @@
     start_load.start()
     mat_load = pltpu.make_async_copy(matrices.at[:, e], mat_v, load_sem.at[1])
     mat_load.start()
+    small_loads = [
+        pltpu.make_async_copy(a, b, load_sem.at[2 + i])
+        for i, (a, b) in enumerate(
+            ((energy_h, energy), (potential_h, potential), (radial_h, radial), (pattern_h, pattern))
+        )
+    ]
+    for load in small_loads:
+        load.start()
     w_loads = [pltpu.make_async_copy(coupling.at[i], raw.at[i], w_sem.at[i]) for i in range(9)]
     for load in w_loads:
         load.start()
@@ -67,16 +107,10 @@
     def _():
         pl.semaphore_signal(barrier, inc=1, device_id=(far, q), device_id_type=MESH)
 
-    def rows_of(i):
-        return pl.ds(pl.multiple_of((i // 2) * 2 * PART, 2 * PART), 2 * PART)
-
-    def lanes_of(i):
-        return pl.ds(pl.multiple_of((i % 2) * HALF, HALF), HALF)
-
     def in_copy(phase, d):
         i = peer(d)
         return pltpu.make_async_remote_copy(
-            src_ref=vt.at[phase, rows_of(i), lanes_of(i)],
+            src_ref=qin.at[phase, i],
             dst_ref=rin.at[phase, g],
             send_sem=in_send.at[phase, d],
             recv_sem=in_recv.at[phase, d],
@@ -87,8 +121,8 @@
     def out_copy(phase, d):
         i = peer(d)
         return pltpu.make_async_remote_copy(
-            src_ref=rout.at[phase, i],
-            dst_ref=vback.at[phase, rows_of(g), lanes_of(g)],
+            src_ref=qout.at[phase, i],
+            dst_ref=rback.at[phase, g],
             send_sem=out_send.at[phase, d],
             recv_sem=out_recv.at[phase, d],
             device_id=(s, e * GROUP + i),
@@ -117,9 +151,13 @@
         )
 
     def send_in(phase):
+        for i in range(GROUP):
+            n, lanes = i // 2, slice((i % 2) * HALF, (i % 2 + 1) * HALF)
+            a, b, c = n * 2 * PART, n * 2 * PART + PART, (n + 1) * 2 * PART
+            pack(v[a:b, lanes], v[b:c, lanes], qin.at[phase, i])
         for d in range(1, GROUP):
             in_copy(phase, d).start()
-        rin[phase, g] = vt[phase, rows_of(g), lanes_of(g)]
+        rin[phase, g] = qin[phase, g]
 
     def send_far(t, j):
         @pl.when(has_far)
@@ -136,10 +174,12 @@
     live = jnp.where(lane < counts[0], 1.0, 0.0).astype(F32)
     for j in range(CH // TILE):
         cols = slice(j * TILE, (j + 1) * TILE)
-        vt[0, :, cols] = start_v[cols, :].T * live[:, cols]
+        v[:, cols] = start_v[cols, :].T * live[:, cols]
     pl.semaphore_wait(barrier, jnp.where(has_far, GROUP + 1, GROUP))
     send_in(0)
 
+    for load in small_loads:
+        load.wait()
     mat_load.wait()
     m0, m1 = mat_v[0], mat_v[1]
     for r, (x, y) in enumerate(((m0, -m1), (m1, m0))):
@@ -154,7 +194,7 @@
         cosine[:, j * TILE : (j + 1) * TILE] = jnp.cos(angle)
         sine[:, j * TILE : (j + 1) * TILE] = jnp.sin(angle)
     for l in range(ORDERS):
-        rad_t[l] = jnp.broadcast_to(radial[l : l + 1, :], (TILE, TILE)).T
+        rad_t[l] = jnp.concatenate([jnp.broadcast_to(radial[l : l + 1, :], (TILE, PART)).T] * (COLS // PART), axis=0)
 
     @pl.when(jnp.logical_not(has_far))
     def _():
@@ -168,7 +208,7 @@
             pltpu.make_async_copy(coupling.at[i], raw.at[i], w_sem.at[i]).wait()
             for a in range(CH // TILE):
                 for b in range(CH // TILE):
-                    keep = jnp.full((TILE, TILE), pattern[a, k, b].astype(F32), F32).astype(BF16)
+                    keep = jnp.full((TILE, TILE), pattern[a, k, 0, b].astype(F32), F32).astype(BF16)
                     tile = raw[i, a * TILE : (a + 1) * TILE, b * TILE : (b + 1) * TILE]
                     wt[
                         k,
@@ -193,21 +233,26 @@
     def radial_phase(phase):
         for d in range(1, GROUP):
             in_copy(phase, d).wait_recv()
-        block = rin[phase].reshape(GROUP, 2, PART, HALF)
-        re = block[:, 0].reshape(GROUP * PART, HALF)
-        im = block[:, 1].reshape(GROUP * PART, HALF)
+        blocks = [unpack(rin.at[phase, i]) for i in range(GROUP)]
+        re = jnp.concatenate([b[0] for b in blocks], axis=0)
+        im = jnp.concatenate([b[1] for b in blocks], axis=0)
         re, im = element(*turn(re, im))
         if phase == 1:
             re, im = element(*turn(re, im))
-        rout[phase, :, :PART, :] = re.reshape(GROUP, PART, HALF)
-        rout[phase, :, PART:, :] = im.reshape(GROUP, PART, HALF)
+        for i in range(GROUP):
+            rows = slice(i * PART, (i + 1) * PART)
+            pack(re[rows], im[rows], qout.at[phase, i])
         for d in range(1, GROUP):
             out_copy(phase, d).start()
-        vback[phase, rows_of(g), lanes_of(g)] = rout[phase, g]
+        rback[phase, g] = qout[phase, g]
 
     def wait_back(phase):
         for d in range(1, GROUP):
             out_copy(phase, d).wait_recv()
+        for i in range(GROUP):
+            n, lanes = i // 2, slice((i % 2) * HALF, (i % 2 + 1) * HALF)
+            a, b, c = n * 2 * PART, n * 2 * PART + PART, (n + 1) * 2 * PART
+            v[a:b, lanes], v[b:c, lanes] = unpack(rback.at[phase, i])
 
     def term(t, scale, emit):
         acc[...] = jnp.dot(xbuf[t, SELF], wt[1], preferred_element_type=F32)
@@ -234,9 +279,8 @@
             emit(j, jnp.where(lane < counts[0], total * scale, 0.0))
 
     def coupling_step(step):
-        phase = step
         base = 3 * step
-        xbuf[base, SELF] = vback[phase].astype(BF16)
+        xbuf[base, SELF] = v[...].astype(BF16)
         for j in range(3):
             send_far(base, j)
         near_copy(base).start()
@@ -249,7 +293,7 @@
 
         def second(j, u):
             lanes = slice(j * FINE, (j + 1) * FINE)
-            even[:, lanes] = vback[phase, :, lanes] - u
+            even[:, lanes] = v[:, lanes] - u
             xbuf[base + 2, SELF, :, lanes] = u.astype(BF16)
             send_far(base + 2, j)
 
@@ -259,8 +303,8 @@
             ev = even[:, lanes]
             for n in range(COLS // (2 * PART)):
                 a, b, c = n * 2 * PART, n * 2 * PART + PART, (n + 1) * 2 * PART
-                vt[phase + 1, a:b, lanes] = ev[a:b] + o[b:c]
-                vt[phase + 1, b:c, lanes] = ev[b:c] - o[a:b]
+                v[a:b, lanes] = ev[a:b] + o[b:c]
+                v[b:c, lanes] = ev[b:c] - o[a:b]
 
         term(base, STEP, first)
         near_copy(base + 1).start()
@@ -282,7 +326,7 @@
     wait_back(2)
     for j in range(CH // TILE):
         cols = slice(j * TILE, (j + 1) * TILE)
-        out[cols, :] = vback[2, :, cols].T
+        out[cols, :] = v[:, cols].T
 
     for phase in range(PHASES):
         for d in range(1, GROUP):
@@ -302,24 +346,24 @@
 ):
     start = start_amplitudes.reshape(CH, COLS)
     weights = coupling[0].transpose(0, 2, 1, 3).reshape(9, CH, CH)
-    radial = jnp.tile(radial_terms, (1, COLS // PART))
     vmem = pl.BlockSpec(memory_space=pltpu.VMEM)
     smem = pl.BlockSpec(memory_space=pltpu.SMEM)
-    anywhere = pl.BlockSpec(memory_space=pl.ANY)
+    anywhere = pl.BlockSpec(memory_space=pltpu.HBM)
     dma = pltpu.SemaphoreType.DMA
     out = pl.pallas_call(
         kernel,
         out_shape=jax.ShapeDtypeStruct((CH, COLS), F32),
-        in_specs=[smem, smem, anywhere, anywhere, vmem, vmem, vmem, anywhere],
+        in_specs=[smem] + [anywhere] * 7,
         out_specs=vmem,
         scratch_shapes=[
             pltpu.VMEM((9, CH, CH), BF16),
             pltpu.VMEM((3, CH, ORDERS * CH), BF16),
             pltpu.VMEM((TERMS, 3, COLS, CH), BF16),
-            pltpu.VMEM((PHASES, GROUP, 2 * PART, HALF), F32),
-            pltpu.VMEM((PHASES, GROUP, 2 * PART, HALF), F32),
-            pltpu.VMEM((PHASES, COLS, CH), F32),
-            pltpu.VMEM((PHASES, COLS, CH), F32),
+            pltpu.VMEM((PHASES, GROUP, BLOCK, PART, TILE), jnp.int16),
+            pltpu.VMEM((PHASES, GROUP, BLOCK, PART, TILE), jnp.int16),
+            pltpu.VMEM((PHASES, GROUP, BLOCK, PART, TILE), jnp.int16),
+            pltpu.VMEM((PHASES, GROUP, BLOCK, PART, TILE), jnp.int16),
+            pltpu.VMEM((COLS, CH), F32),
             pltpu.VMEM((COLS, ORDERS * CH), F32),
             pltpu.VMEM((COLS, CH), F32),
             pltpu.VMEM((COLS, CH), F32),
@@ -330,7 +374,11 @@
             pltpu.VMEM((2 * TILE, 2 * TILE), BF16),
             pltpu.VMEM((2 * TILE, 2 * TILE), BF16),
             pltpu.VMEM((ORDERS, TILE, TILE), F32),
-            dma((2,)),
+            pltpu.SMEM((6, 3, 1, 6), jnp.int32),
+            pltpu.VMEM((3, PART), F32),
+            pltpu.VMEM((1, CH), F32),
+            pltpu.VMEM((4, TILE), F32),
+            dma((6,)),
             dma((9,)),
             dma((PHASES, GROUP)),
             dma((PHASES, GROUP)),
@@ -342,14 +390,14 @@
             dma((TERMS, 3)),
         ],
         compiler_params=pltpu.CompilerParams(
-            collective_id=0, has_side_effects=True, vmem_limit_bytes=52 * 2**20
+            collective_id=0, has_side_effects=True, vmem_limit_bytes=48 * 2**20
         ),
     )(
         counts,
-        block_pattern[0],
+        block_pattern.transpose(1, 2, 0, 3),
         start,
         weights,
-        radial,
+        radial_terms,
         energy,
         potential.reshape(4, TILE),
         element_matrices,

time: 95.5 us -> 88.6 us (0.928)
  the two profiles are of different devices: /device:TPU:1 before, /device:TPU:65 now
where the time goes in v1:
time: 88.6 us; the launch traced here: 88.3 us
  Pallas kernels  82.1 us (93%)
  local copies, waits for them, and re-layouts  5.52 us (6%)
    pallas_call x1, Pallas kernels, shards(): pl.pallas_call(kernel, out_shape=jax.ShapeDtypeStruct((CH, COLS), F32), i...  82.1 us
    unnamed x13, local copies, waits for them, and re-layouts  5.52 us

profile of v1, /device:TPU:65, one launch (start us, length us, event | category | flops | bytes accessed | tf_op | source)
XLA Modules:
  0.0 88.3 jit_solution(4686075724283854339)
XLA Ops:
  0.7 0.0 copy-start
  0.7 1.0 %copy-done = f32[2,4,128,128]{3,2,1,0:T(8,128)S(1)} copy-done((f32[2,4,128,128]{3,2,1,0:T(8,128)S(1)}, f32[2,4,128,128]{3,2,1,0:T(8,128)}, u32[]{:S(2)}) %copy-start) | copy-done | bytes 524312
  1.7 0.0 copy-start.1
  1.7 1.0 %copy-done.1 = f32[1,768,1,128]{3,2,1,0:T(1,128)S(1)} copy-done((f32[1,768,1,128]{3,2,1,0:T(1,128)S(1)}, f32[1,768,1,128]{3,2,1,0:T(1,128)}, u32[]{:S(2)}) %copy-start.1) | copy-done | bytes 393240
  2.7 0.0 copy-start.2
  2.7 0.7 copy-done.2
  3.4 0.0 copy-start.3
  3.4 0.7 copy-done.3
  4.1 0.0 copy-start.4
  4.1 0.7 copy-done.4
  4.8 0.0 copy-start.5
  4.8 0.7 copy-done.5
  5.4 82.1 %shard_map.82 = f32[768,128]{1,0:T(8,128)S(1)} custom-call(s32[1]{0:T(128)S(6)} %copy.11.counts, s32[6,3,1,6]{3,2,1,0:T(1,128)S(1)} %bitcast.13, f32[768,128]{1,0:T(8,128)S(1)} %bitcast.12, bf16[9,768,768]{2,1,0:T(8,128)(2,1)} %bitcast.15, f32[3,16]{1,0:T(4,128)S(1)} %copy-done.4, f32[1,768]{1,0:T(1,128)S(1)} %copy-done.3, f32[4,128]{1,0:T(4,128)S(1)} %bitcast.14, ...), custom_call_target="tpu_custom_call" | custom-call | tf_op jit(solution)/shard_map/pallas_call | solution.py:353
  87.6 0.7 copy.12
Async XLA Ops:
  0.7 1.0 %copy-start = (f32[2,4,128,128]{3,2,1,0:T(8,128)S(1)}, f32[2,4,128,128]{3,2,1,0:T(8,128)}, u32[]{:S(2)}) copy-start(f32[2,4,128,128]{3,2,1,0:T(8,128)} %matrices.1) | copy-start | bytes 1572868
  1.7 1.0 %copy-start.1 = (f32[1,768,1,128]{3,2,1,0:T(1,128)S(1)}, f32[1,768,1,128]{3,2,1,0:T(1,128)}, u32[]{:S(2)}) copy-start(f32[1,768,1,128]{3,2,1,0:T(1,128)} %param.8) | copy-start | bytes 1179652
  2.7 0.7 copy-start.2
  3.4 0.7 copy-start.3
  4.1 0.7 copy-start.4
  4.8 0.7 copy-start.5

commit v2 on v1

--- a/solution.py
+++ b/solution.py
@@ -23,8 +23,19 @@
 BLOCK = 7
 LEVELS = 64.0
 FULL = 32760.0
+PARTS = ((0, 2), (2, 4))
 F32 = jnp.float32
 BF16 = jnp.bfloat16
+
+
+def rows_in(part):
+    first, last = PARTS[part]
+    return pl.ds(first * 2 * PART, (last - first) * 2 * PART)
+
+
+def devices_in(part):
+    first, last = PARTS[part]
+    return range(2 * first, 2 * last)
 
 
 def split(x):
@@ -62,8 +73,9 @@
 def kernel(
     counts, pattern_h, start, coupling, radial_h, energy_h, potential_h, matrices,
     out,
-    raw, wt, xbuf, qin, rin, qout, rback, v, acc, even, odd, cosine, sine, start_v, mat_v, bhigh, blow, rad_t,
-    pattern, radial, energy, potential, load_sem, w_sem, in_send, in_recv, out_send, out_recv, near_send, near_recv, far_send, far_recv,
+    raw, wt, xbuf, hout, qin, rin, qout, rback, v, acc, even, odd, cosine, sine, start_v, mat_v, bhigh, blow, rad_t,
+    pattern, radial, energy, potential, load_sem, w_sem, in_send, in_recv, out_send, out_recv, near_send, near_recv,
+    far_send, far_recv, direct_send, direct_recv,
 ):
     s = lax.axis_index("sym")
     q = lax.axis_index("rad")
@@ -92,82 +104,99 @@
     for load in w_loads:
         load.start()
 
-    def peer(d):
-        return (g + d) % GROUP
-
-    def peer_back(d):
-        return (g + GROUP - d) % GROUP
-
     barrier = pltpu.get_barrier_semaphore()
     for d in range(1, GROUP):
-        pl.semaphore_signal(barrier, inc=1, device_id=(s, e * GROUP + peer(d)), device_id_type=MESH)
+        pl.semaphore_signal(
+            barrier, inc=1, device_id=(s, e * GROUP + (g + d) % GROUP), device_id_type=MESH
+        )
     pl.semaphore_signal(barrier, inc=1, device_id=(near, q), device_id_type=MESH)
 
     @pl.when(has_far)
     def _():
         pl.semaphore_signal(barrier, inc=1, device_id=(far, q), device_id_type=MESH)
 
-    def in_copy(phase, d):
-        i = peer(d)
+    def in_copy(phase, i):
         return pltpu.make_async_remote_copy(
             src_ref=qin.at[phase, i],
             dst_ref=rin.at[phase, g],
-            send_sem=in_send.at[phase, d],
-            recv_sem=in_recv.at[phase, d],
+            send_sem=in_send.at[phase, i],
+            recv_sem=in_recv.at[phase, g],
             device_id=(s, e * GROUP + i),
             device_id_type=MESH,
         )
 
-    def out_copy(phase, d):
-        i = peer(d)
+    def out_copy(phase, i):
         return pltpu.make_async_remote_copy(
             src_ref=qout.at[phase, i],
             dst_ref=rback.at[phase, g],
-            send_sem=out_send.at[phase, d],
-            recv_sem=out_recv.at[phase, d],
+            send_sem=out_send.at[phase, i],
+            recv_sem=out_recv.at[phase, g],
             device_id=(s, e * GROUP + i),
             device_id_type=MESH,
         )
 
-    def near_copy(t):
+    def wait_block(recv_sem, ref, i):
+        @pl.when(g != i)
+        def _():
+            pltpu.make_async_copy(ref, ref, recv_sem).wait()
+
+    def rows_of(i):
+        return pl.ds(pl.multiple_of((i // 2) * 2 * PART, 2 * PART), 2 * PART)
+
+    def lanes_of(i):
+        return pl.ds(pl.multiple_of((i % 2) * HALF, HALF), HALF)
+
+    def direct_copy(step, i):
         return pltpu.make_async_remote_copy(
-            src_ref=xbuf.at[t, SELF],
-            dst_ref=xbuf.at[t, NEAR],
-            send_sem=near_send.at[t],
-            recv_sem=near_recv.at[t],
+            src_ref=hout.at[step, i],
+            dst_ref=xbuf.at[3 * step, FAR, rows_of(g), lanes_of(g)],
+            send_sem=direct_send.at[step, i],
+            recv_sem=direct_recv.at[step, g],
+            device_id=(far, e * GROUP + i),
+            device_id_type=MESH,
+        )
+
+    def near_copy(t, part):
+        rows = rows_in(part)
+        return pltpu.make_async_remote_copy(
+            src_ref=xbuf.at[t, SELF, rows],
+            dst_ref=xbuf.at[t, NEAR, rows],
+            send_sem=near_send.at[t, part],
+            recv_sem=near_recv.at[t, part],
             device_id=(near, q),
             device_id_type=MESH,
         )
 
-    def far_copy(t, j):
+    def far_copy(t, part, j):
+        rows = rows_in(part)
         lanes = pl.ds(j * FINE, FINE)
         return pltpu.make_async_remote_copy(
-            src_ref=xbuf.at[t, SELF, :, lanes],
-            dst_ref=xbuf.at[t, FAR, :, lanes],
-            send_sem=far_send.at[t, j],
-            recv_sem=far_recv.at[t, j],
+            src_ref=xbuf.at[t, SELF, rows, lanes],
+            dst_ref=xbuf.at[t, FAR, rows, lanes],
+            send_sem=far_send.at[t, part, j],
+            recv_sem=far_recv.at[t, part, j],
             device_id=(far, q),
             device_id_type=MESH,
         )
 
-    def send_in(phase):
-        for i in range(GROUP):
+    def send_in(phase, part):
+        for i in devices_in(part):
             n, lanes = i // 2, slice((i % 2) * HALF, (i % 2 + 1) * HALF)
             a, b, c = n * 2 * PART, n * 2 * PART + PART, (n + 1) * 2 * PART
             pack(v[a:b, lanes], v[b:c, lanes], qin.at[phase, i])
-        for d in range(1, GROUP):
-            in_copy(phase, d).start()
-        rin[phase, g] = qin[phase, g]
-
-    def send_far(t, j):
+
+            @pl.when(g != i)
+            def _():
+                in_copy(phase, i).start()
+
+            @pl.when(g == i)
+            def _():
+                rin[phase, i] = qin[phase, i]
+
+    def send_far(t, part, j):
         @pl.when(has_far)
         def _():
-            far_copy(t, j).start()
-
-    def wait_far(t, j):
-        @pl.when(has_far)
-        def _():
-            far_copy(t, j).wait_recv()
+            far_copy(t, part, j).start()
 
     start_load.wait()
     lane = lax.broadcasted_iota(jnp.int32, (COLS, CH), 1)
@@ -176,7 +205,8 @@
         cols = slice(j * TILE, (j + 1) * TILE)
         v[:, cols] = start_v[cols, :].T * live[:, cols]
     pl.semaphore_wait(barrier, jnp.where(has_far, GROUP + 1, GROUP))
-    send_in(0)
+    for part in range(len(PARTS)):
+        send_in(0, part)
 
     for load in small_loads:
         load.wait()
@@ -231,8 +261,8 @@
         return re * c + im * n, im * c - re * n
 
     def radial_phase(phase):
-        for d in range(1, GROUP):
-            in_copy(phase, d).wait_recv()
+        for i in range(GROUP):
+            wait_block(in_recv.at[phase, i], rin.at[phase, i], i)
         blocks = [unpack(rin.at[phase, i]) for i in range(GROUP)]
         re = jnp.concatenate([b[0] for b in blocks], axis=0)
         im = jnp.concatenate([b[1] for b in blocks], axis=0)
@@ -241,104 +271,130 @@
             re, im = element(*turn(re, im))
         for i in range(GROUP):
             rows = slice(i * PART, (i + 1) * PART)
+            if phase < 2:
+                hout[phase, i, :PART] = re[rows].astype(BF16)
+                hout[phase, i, PART:] = im[rows].astype(BF16)
+
+                @pl.when(has_far)
+                def _():
+                    direct_copy(phase, i).start()
+
             pack(re[rows], im[rows], qout.at[phase, i])
-        for d in range(1, GROUP):
-            out_copy(phase, d).start()
-        rback[phase, g] = qout[phase, g]
-
-    def wait_back(phase):
-        for d in range(1, GROUP):
-            out_copy(phase, d).wait_recv()
-        for i in range(GROUP):
+
+            @pl.when(g != i)
+            def _():
+                out_copy(phase, i).start()
+
+            @pl.when(g == i)
+            def _():
+                rback[phase, i] = qout[phase, i]
+
+    def wait_back(phase, part):
+        for i in devices_in(part):
+            wait_block(out_recv.at[phase, i], rback.at[phase, i], i)
             n, lanes = i // 2, slice((i % 2) * HALF, (i % 2 + 1) * HALF)
             a, b, c = n * 2 * PART, n * 2 * PART + PART, (n + 1) * 2 * PART
             v[a:b, lanes], v[b:c, lanes] = unpack(rback.at[phase, i])
 
-    def term(t, scale, emit):
+    def wait_far(t, part):
+        @pl.when(has_far)
+        def _():
+            if t % 3 == 0:
+                for i in devices_in(part):
+                    ref = hout.at[t // 3, i]
+                    pltpu.make_async_copy(ref, ref, direct_recv.at[t // 3, i]).wait()
+            else:
+                for j in range(CH // FINE):
+                    far_copy(t, part, j).wait_recv()
+
+    def term(t, scale, emit, after):
         acc[...] = jnp.dot(xbuf[t, SELF], wt[1], preferred_element_type=F32)
-        near_copy(t).wait_recv()
+        for part in range(len(PARTS)):
+            near_copy(t, part).wait_recv()
         acc[...] += jnp.dot(xbuf[t, NEAR], wt[k_near], preferred_element_type=F32)
-        wait_far(t, 0)
-        wait_far(t, 1)
-        acc[...] += jnp.dot(
-            xbuf[t, FAR, :, : 2 * FINE], wt[k_far, : 2 * FINE], preferred_element_type=F32
-        )
-        wait_far(t, 2)
-        for j in range(CH // FINE):
-            total = None
-            for l in range(ORDERS):
-                lanes = slice(l * CH + j * FINE, l * CH + (j + 1) * FINE)
-                y = acc[:, lanes] + jnp.dot(
-                    xbuf[t, FAR, :, 2 * FINE :],
-                    wt[k_far, 2 * FINE :, lanes],
-                    preferred_element_type=F32,
-                )
-                factor = jnp.concatenate((rad_t[l], rad_t[l]), axis=1)
-                total = y * factor if total is None else total + y * factor
-            lane = lax.broadcasted_iota(jnp.int32, (COLS, FINE), 1) + j * FINE
-            emit(j, jnp.where(lane < counts[0], total * scale, 0.0))
+        for part in range(len(PARTS)):
+            rows = slice(PARTS[part][0] * 2 * PART, PARTS[part][1] * 2 * PART)
+            count = rows.stop - rows.start
+            wait_far(t, part)
+            for j in range(CH // FINE):
+                total = None
+                for l in range(ORDERS):
+                    lanes = slice(l * CH + j * FINE, l * CH + (j + 1) * FINE)
+                    y = acc[rows, lanes] + jnp.dot(
+                        xbuf[t, FAR, rows, :], wt[k_far, :, lanes], preferred_element_type=F32
+                    )
+                    factor = jnp.concatenate((rad_t[l, :count], rad_t[l, :count]), axis=1)
+                    total = y * factor if total is None else total + y * factor
+                lane = lax.broadcasted_iota(jnp.int32, (count, FINE), 1) + j * FINE
+                lanes = slice(j * FINE, (j + 1) * FINE)
+                emit(part, rows, j, lanes, jnp.where(lane < counts[0], total * scale, 0.0))
+            after(part)
 
     def coupling_step(step):
         base = 3 * step
-        xbuf[base, SELF] = v[...].astype(BF16)
-        for j in range(3):
-            send_far(base, j)
-        near_copy(base).start()
-
-        def first(j, u):
-            lanes = slice(j * FINE, (j + 1) * FINE)
-            odd[:, lanes] = u
-            xbuf[base + 1, SELF, :, lanes] = u.astype(BF16)
-            send_far(base + 1, j)
-
-        def second(j, u):
-            lanes = slice(j * FINE, (j + 1) * FINE)
-            even[:, lanes] = v[:, lanes] - u
-            xbuf[base + 2, SELF, :, lanes] = u.astype(BF16)
-            send_far(base + 2, j)
-
-        def third(j, u):
-            lanes = slice(j * FINE, (j + 1) * FINE)
-            o = odd[:, lanes] - u
-            ev = even[:, lanes]
-            for n in range(COLS // (2 * PART)):
+        for part in range(len(PARTS)):
+            wait_back(step, part)
+            rows = rows_in(part)
+            xbuf[base, SELF, rows] = v[rows].astype(BF16)
+            near_copy(base, part).start()
+
+        def first(part, rows, j, lanes, u):
+            odd[rows, lanes] = u
+            xbuf[base + 1, SELF, rows, lanes] = u.astype(BF16)
+            send_far(base + 1, part, j)
+
+        def second(part, rows, j, lanes, u):
+            even[rows, lanes] = v[rows, lanes] - u
+            xbuf[base + 2, SELF, rows, lanes] = u.astype(BF16)
+            send_far(base + 2, part, j)
+
+        def third(part, rows, j, lanes, u):
+            o = odd[rows, lanes] - u
+            ev = even[rows, lanes]
+            for n in range(u.shape[0] // (2 * PART)):
                 a, b, c = n * 2 * PART, n * 2 * PART + PART, (n + 1) * 2 * PART
-                v[a:b, lanes] = ev[a:b] + o[b:c]
-                v[b:c, lanes] = ev[b:c] - o[a:b]
-
-        term(base, STEP, first)
-        near_copy(base + 1).start()
-        term(base + 1, STEP / 2.0, second)
-        near_copy(base + 2).start()
-        term(base + 2, STEP / 3.0, third)
+                v[rows.start + a : rows.start + b, lanes] = ev[a:b] + o[b:c]
+                v[rows.start + b : rows.start + c, lanes] = ev[b:c] - o[a:b]
+
+        term(base, STEP, first, lambda part: near_copy(base + 1, part).start())
+        term(base + 1, STEP / 2.0, second, lambda part: near_copy(base + 2, part).start())
+        term(base + 2, STEP / 3.0, third, lambda part: send_in(step + 1, part))
 
     turn_weights(0, 5)
     radial_phase(0)
     turn_weights(5, 9)
-    wait_back(0)
     coupling_step(0)
-    send_in(1)
     radial_phase(1)
-    wait_back(1)
     coupling_step(1)
-    send_in(2)
     radial_phase(2)
-    wait_back(2)
+    for part in range(len(PARTS)):
+        wait_back(2, part)
     for j in range(CH // TILE):
         cols = slice(j * TILE, (j + 1) * TILE)
         out[cols, :] = v[:, cols].T
 
     for phase in range(PHASES):
-        for d in range(1, GROUP):
-            in_copy(phase, d).wait_send()
-            out_copy(phase, d).wait_send()
+        for i in range(GROUP):
+
+            @pl.when(g != i)
+            def _():
+                in_copy(phase, i).wait_send()
+                out_copy(phase, i).wait_send()
+
     for t in range(TERMS):
-        near_copy(t).wait_send()
-
-        @pl.when(has_far)
-        def _():
-            for j in range(3):
-                far_copy(t, j).wait_send()
+        for part in range(len(PARTS)):
+            near_copy(t, part).wait_send()
+
+    @pl.when(has_far)
+    def _():
+        for step in range(2):
+            for i in range(GROUP):
+                direct_copy(step, i).wait_send()
+        for t in range(TERMS):
+            if t % 3:
+                for part in range(len(PARTS)):
+                    for j in range(CH // FINE):
+                        far_copy(t, part, j).wait_send()
 
 
 def shards(
@@ -359,6 +415,7 @@
             pltpu.VMEM((9, CH, CH), BF16),
             pltpu.VMEM((3, CH, ORDERS * CH), BF16),
             pltpu.VMEM((TERMS, 3, COLS, CH), BF16),
+            pltpu.VMEM((2, GROUP, 2 * PART, HALF), BF16),
             pltpu.VMEM((PHASES, GROUP, BLOCK, PART, TILE), jnp.int16),
             pltpu.VMEM((PHASES, GROUP, BLOCK, PART, TILE), jnp.int16),
             pltpu.VMEM((PHASES, GROUP, BLOCK, PART, TILE), jnp.int16),
@@ -384,13 +441,15 @@
             dma((PHASES, GROUP)),
             dma((PHASES, GROUP)),
             dma((PHASES, GROUP)),
-            dma((TERMS,)),
-            dma((TERMS,)),
-            dma((TERMS, 3)),
-            dma((TERMS, 3)),
+            dma((TERMS, len(PARTS))),
+            dma((TERMS, len(PARTS))),
+            dma((TERMS, len(PARTS), CH // FINE)),
+            dma((TERMS, len(PARTS), CH // FINE)),
+            dma((2, GROUP)),
+            dma((2, GROUP)),
         ],
         compiler_params=pltpu.CompilerParams(
-            collective_id=0, has_side_effects=True, vmem_limit_bytes=48 * 2**20
+            collective_id=0, has_side_effects=True, vmem_limit_bytes=60 * 2**20
         ),
     )(
         counts,

time: 88.6 us -> 80.2 us (0.905)
  the two profiles are of different devices: /device:TPU:65 before, /device:TPU:64 now
where the time goes in v2:
time: 80.2 us; the launch traced here: 80.1 us
  Pallas kernels  77.6 us (97%)
  local copies, waits for them, and re-layouts  1.77 us (2%)
    pallas_call x1, Pallas kernels, shards(): pl.pallas_call(kernel, out_shape=jax.ShapeDtypeStruct((CH, COLS), F32), i...  77.6 us
    unnamed x1, local copies, waits for them, and re-layouts  1.77 us

profile of v2, /device:TPU:64, one launch (start us, length us, event | category | flops | bytes accessed | tf_op | source)
XLA Modules:
  0.0 80.1 jit_solution(11113542092744460926)
XLA Ops:
  0.7 77.6 %shard_map.82 = f32[768,128]{1,0:T(8,128)} custom-call(s32[1]{0:T(128)S(6)} %copy.11.counts, s32[6,3,1,6]{3,2,1,0:T(1,128)} %bitcast.14, f32[768,128]{1,0:T(8,128)} %bitcast.13, bf16[9,768,768]{2,1,0:T(8,128)(2,1)} %bitcast.11, f32[3,16]{1,0:T(4,128)} %radial_h.1, f32[1,768]{1,0:T(1,128)} %energy_h.1, f32[4,128]{1,0:T(4,128)} %bitcast.15, ...), custom_call_target="tpu_custom_call" | custom-call | tf_op jit(solution)/shard_map/pallas_call | solution.py:409
  78.3 1.8 %copy.12 = f32[1,768,1,128]{3,2,1,0:T(1,128)} copy(f32[1,768,1,128]{3,2,1,0:T(1,128)} %bitcast.12) | data formatting | bytes 786432

commit v3 on v2

--- a/solution.py
+++ b/solution.py
@@ -23,19 +23,12 @@
 BLOCK = 7
 LEVELS = 64.0
 FULL = 32760.0
-PARTS = ((0, 2), (2, 4))
+PARTS = 2
+ROWS = COLS // PARTS
+STATES = ROWS // (2 * PART)
+BLOCKS = GROUP // PARTS
 F32 = jnp.float32
 BF16 = jnp.bfloat16
-
-
-def rows_in(part):
-    first, last = PARTS[part]
-    return pl.ds(first * 2 * PART, (last - first) * 2 * PART)
-
-
-def devices_in(part):
-    first, last = PARTS[part]
-    return range(2 * first, 2 * last)
 
 
 def split(x):
@@ -73,7 +66,7 @@
 def kernel(
     counts, pattern_h, start, coupling, radial_h, energy_h, potential_h, matrices,
     out,
-    raw, wt, xbuf, hout, qin, rin, qout, rback, v, acc, even, odd, cosine, sine, start_v, mat_v, bhigh, blow, rad_t,
+    raw, wt, xbuf, hout, qin, rin, qout, rback, v, acc, odd, turned, cosine, sine, start_v, mat_v, bhigh, blow, rad_t,
     pattern, radial, energy, potential, load_sem, w_sem, in_send, in_recv, out_send, out_recv, near_send, near_recv,
     far_send, far_recv, direct_send, direct_recv,
 ):
@@ -156,6 +149,9 @@
             device_id_type=MESH,
         )
 
+    def rows_in(part):
+        return pl.ds(pl.multiple_of(part * ROWS, ROWS), ROWS)
+
     def near_copy(t, part):
         rows = rows_in(part)
         return pltpu.make_async_remote_copy(
@@ -167,23 +163,32 @@
             device_id_type=MESH,
         )
 
-    def far_copy(t, part, j):
+    def far_copy(t, part):
         rows = rows_in(part)
-        lanes = pl.ds(j * FINE, FINE)
         return pltpu.make_async_remote_copy(
-            src_ref=xbuf.at[t, SELF, rows, lanes],
-            dst_ref=xbuf.at[t, FAR, rows, lanes],
-            send_sem=far_send.at[t, part, j],
-            recv_sem=far_recv.at[t, part, j],
+            src_ref=xbuf.at[t, SELF, rows],
+            dst_ref=xbuf.at[t, FAR, rows],
+            send_sem=far_send.at[t, part],
+            recv_sem=far_recv.at[t, part],
             device_id=(far, q),
             device_id_type=MESH,
         )
 
+    def block_at(part, b):
+        first = pl.multiple_of(part * ROWS, ROWS) + (b // 2) * 2 * PART
+        lanes = slice((b % 2) * HALF, (b % 2 + 1) * HALF)
+        real = pl.ds(pl.multiple_of(first, PART), PART)
+        imag = pl.ds(pl.multiple_of(first + PART, PART), PART)
+        return part * BLOCKS + b, real, imag, lanes
+
     def send_in(phase, part):
-        for i in devices_in(part):
-            n, lanes = i // 2, slice((i % 2) * HALF, (i % 2 + 1) * HALF)
-            a, b, c = n * 2 * PART, n * 2 * PART + PART, (n + 1) * 2 * PART
-            pack(v[a:b, lanes], v[b:c, lanes], qin.at[phase, i])
+        for b in range(BLOCKS):
+            i, real, imag, lanes = block_at(part, b)
+            pack(
+                v[real, lanes] + odd[imag, lanes],
+                v[imag, lanes] - odd[real, lanes],
+                qin.at[phase, i],
+            )
 
             @pl.when(g != i)
             def _():
@@ -192,11 +197,6 @@
             @pl.when(g == i)
             def _():
                 rin[phase, i] = qin[phase, i]
-
-    def send_far(t, part, j):
-        @pl.when(has_far)
-        def _():
-            far_copy(t, part, j).start()
 
     start_load.wait()
     lane = lax.broadcasted_iota(jnp.int32, (COLS, CH), 1)
@@ -205,8 +205,13 @@
         cols = slice(j * TILE, (j + 1) * TILE)
         v[:, cols] = start_v[cols, :].T * live[:, cols]
     pl.semaphore_wait(barrier, jnp.where(has_far, GROUP + 1, GROUP))
-    for part in range(len(PARTS)):
+    odd[...] = jnp.zeros_like(odd)
+
+    def send_first(part, _):
         send_in(0, part)
+        return 0
+
+    lax.fori_loop(0, PARTS, send_first, 0)
 
     for load in small_loads:
         load.wait()
@@ -228,8 +233,11 @@
 
     @pl.when(jnp.logical_not(has_far))
     def _():
-        for t in range(TERMS):
+        def clear(t, _):
             xbuf[t, FAR] = jnp.zeros((COLS, CH), BF16)
+            return 0
+
+        lax.fori_loop(0, TERMS, clear, 0)
 
     def turn_weights(first, last):
         def body(i, _):
@@ -249,37 +257,35 @@
 
         lax.fori_loop(first, last, body, 0)
 
-    def element(re, im):
-        xhigh, xlow = split(jnp.concatenate((re, im), axis=0))
+    def radial_step(_, carry):
+        re, im = turned[:128], turned[128:]
+        c, n = cosine[...], sine[...]
+        xhigh, xlow = split(jnp.concatenate((re * c + im * n, im * c - re * n), axis=0))
         y = jnp.dot(bhigh[...], xhigh, preferred_element_type=F32)
         y = y + jnp.dot(bhigh[...], xlow, preferred_element_type=F32)
-        y = y + jnp.dot(blow[...], xhigh, preferred_element_type=F32)
-        return y[:128], y[128:]
-
-    def turn(re, im):
-        c, n = cosine[...], sine[...]
-        return re * c + im * n, im * c - re * n
+        turned[...] = y + jnp.dot(blow[...], xhigh, preferred_element_type=F32)
+        return carry
 
     def radial_phase(phase):
         for i in range(GROUP):
             wait_block(in_recv.at[phase, i], rin.at[phase, i], i)
-        blocks = [unpack(rin.at[phase, i]) for i in range(GROUP)]
-        re = jnp.concatenate([b[0] for b in blocks], axis=0)
-        im = jnp.concatenate([b[1] for b in blocks], axis=0)
-        re, im = element(*turn(re, im))
-        if phase == 1:
-            re, im = element(*turn(re, im))
         for i in range(GROUP):
             rows = slice(i * PART, (i + 1) * PART)
-            if phase < 2:
-                hout[phase, i, :PART] = re[rows].astype(BF16)
-                hout[phase, i, PART:] = im[rows].astype(BF16)
-
-                @pl.when(has_far)
-                def _():
-                    direct_copy(phase, i).start()
-
-            pack(re[rows], im[rows], qout.at[phase, i])
+            turned[i * PART : (i + 1) * PART], turned[128 + i * PART : 128 + (i + 1) * PART] = unpack(
+                rin.at[phase, i]
+            )
+        lax.fori_loop(0, jnp.where(phase == 1, 2, 1), radial_step, 0)
+        for i in range(GROUP):
+            re = turned[i * PART : (i + 1) * PART]
+            im = turned[128 + i * PART : 128 + (i + 1) * PART]
+            hout[phase, i, :PART] = re.astype(BF16)
+            hout[phase, i, PART:] = im.astype(BF16)
+            pack(re, im, qout.at[phase, i])
+
+        def send(i, _):
+            @pl.when(jnp.logical_and(has_far, phase < 2))
+            def _():
+                direct_copy(phase, i).start()
 
             @pl.when(g != i)
             def _():
@@ -289,33 +295,55 @@
             def _():
                 rback[phase, i] = qout[phase, i]
 
-    def wait_back(phase, part):
-        for i in devices_in(part):
-            wait_block(out_recv.at[phase, i], rback.at[phase, i], i)
-            n, lanes = i // 2, slice((i % 2) * HALF, (i % 2 + 1) * HALF)
-            a, b, c = n * 2 * PART, n * 2 * PART + PART, (n + 1) * 2 * PART
-            v[a:b, lanes], v[b:c, lanes] = unpack(rback.at[phase, i])
-
-    def wait_far(t, part):
-        @pl.when(has_far)
+            return 0
+
+        lax.fori_loop(0, GROUP, send, 0)
+
+    def back(phase):
+        def body(part, _):
+            for b in range(BLOCKS):
+                i, real, imag, lanes = block_at(part, b)
+                wait_block(out_recv.at[phase, i], rback.at[phase, i], i)
+            for b in range(BLOCKS):
+                i, real, imag, lanes = block_at(part, b)
+                v[real, lanes], v[imag, lanes] = unpack(rback.at[phase, i])
+            rows = rows_in(part)
+            xbuf[3 * phase, SELF, rows] = v[rows].astype(BF16)
+
+            @pl.when(phase < 2)
+            def _():
+                near_copy(3 * phase, part).start()
+
+            return 0
+
+        lax.fori_loop(0, PARTS, body, 0)
+
+    def wait_far(phase, order, part):
+        @pl.when(jnp.logical_and(has_far, order == 0))
         def _():
-            if t % 3 == 0:
-                for i in devices_in(part):
-                    ref = hout.at[t // 3, i]
-                    pltpu.make_async_copy(ref, ref, direct_recv.at[t // 3, i]).wait()
-            else:
-                for j in range(CH // FINE):
-                    far_copy(t, part, j).wait_recv()
-
-    def term(t, scale, emit, after):
+            for b in range(BLOCKS):
+                i = part * BLOCKS + b
+                ref = hout.at[phase, i]
+                pltpu.make_async_copy(ref, ref, direct_recv.at[phase, i]).wait()
+
+        @pl.when(jnp.logical_and(has_far, order > 0))
+        def _():
+            far_copy(3 * phase + order, part).wait_recv()
+
+    def term(phase, order):
+        t = 3 * phase + order
+        scale = jnp.where(order == 0, STEP, jnp.where(order == 1, STEP / 2.0, STEP / 3.0))
+        keep_odd = jnp.where(order == 0, 0.0, 1.0)
+        add_odd = jnp.where(order == 0, 1.0, jnp.where(order == 1, 0.0, -1.0))
+        add_even = jnp.where(order == 1, -1.0, 0.0)
         acc[...] = jnp.dot(xbuf[t, SELF], wt[1], preferred_element_type=F32)
-        for part in range(len(PARTS)):
+        for part in range(PARTS):
             near_copy(t, part).wait_recv()
         acc[...] += jnp.dot(xbuf[t, NEAR], wt[k_near], preferred_element_type=F32)
-        for part in range(len(PARTS)):
-            rows = slice(PARTS[part][0] * 2 * PART, PARTS[part][1] * 2 * PART)
-            count = rows.stop - rows.start
-            wait_far(t, part)
+
+        def body(part, _):
+            rows = rows_in(part)
+            wait_far(phase, order, part)
             for j in range(CH // FINE):
                 total = None
                 for l in range(ORDERS):
@@ -323,78 +351,85 @@
                     y = acc[rows, lanes] + jnp.dot(
                         xbuf[t, FAR, rows, :], wt[k_far, :, lanes], preferred_element_type=F32
                     )
-                    factor = jnp.concatenate((rad_t[l, :count], rad_t[l, :count]), axis=1)
+                    factor = jnp.concatenate((rad_t[l, :ROWS], rad_t[l, :ROWS]), axis=1)
                     total = y * factor if total is None else total + y * factor
-                lane = lax.broadcasted_iota(jnp.int32, (count, FINE), 1) + j * FINE
+                lane = lax.broadcasted_iota(jnp.int32, (ROWS, FINE), 1) + j * FINE
                 lanes = slice(j * FINE, (j + 1) * FINE)
-                emit(part, rows, j, lanes, jnp.where(lane < counts[0], total * scale, 0.0))
-            after(part)
-
-    def coupling_step(step):
-        base = 3 * step
-        for part in range(len(PARTS)):
-            wait_back(step, part)
-            rows = rows_in(part)
-            xbuf[base, SELF, rows] = v[rows].astype(BF16)
-            near_copy(base, part).start()
-
-        def first(part, rows, j, lanes, u):
-            odd[rows, lanes] = u
-            xbuf[base + 1, SELF, rows, lanes] = u.astype(BF16)
-            send_far(base + 1, part, j)
-
-        def second(part, rows, j, lanes, u):
-            even[rows, lanes] = v[rows, lanes] - u
-            xbuf[base + 2, SELF, rows, lanes] = u.astype(BF16)
-            send_far(base + 2, part, j)
-
-        def third(part, rows, j, lanes, u):
-            o = odd[rows, lanes] - u
-            ev = even[rows, lanes]
-            for n in range(u.shape[0] // (2 * PART)):
-                a, b, c = n * 2 * PART, n * 2 * PART + PART, (n + 1) * 2 * PART
-                v[rows.start + a : rows.start + b, lanes] = ev[a:b] + o[b:c]
-                v[rows.start + b : rows.start + c, lanes] = ev[b:c] - o[a:b]
-
-        term(base, STEP, first, lambda part: near_copy(base + 1, part).start())
-        term(base + 1, STEP / 2.0, second, lambda part: near_copy(base + 2, part).start())
-        term(base + 2, STEP / 3.0, third, lambda part: send_in(step + 1, part))
+                u = jnp.where(lane < counts[0], total * scale, 0.0)
+                odd[rows, lanes] = odd[rows, lanes] * keep_odd + u * add_odd
+                v[rows, lanes] += u * add_even
+                xbuf[t + 1, SELF, rows, lanes] = u.astype(BF16)
+
+            @pl.when(jnp.logical_and(has_far, order < 2))
+            def _():
+                far_copy(t + 1, part).start()
+
+            @pl.when(order < 2)
+            def _():
+                near_copy(t + 1, part).start()
+
+            @pl.when(order == 2)
+            def _():
+                send_in(phase + 1, part)
+
+            return 0
+
+        lax.fori_loop(0, PARTS, body, 0)
 
     turn_weights(0, 5)
-    radial_phase(0)
-    turn_weights(5, 9)
-    coupling_step(0)
-    radial_phase(1)
-    coupling_step(1)
-    radial_phase(2)
-    for part in range(len(PARTS)):
-        wait_back(2, part)
+
+    def one_phase(phase, _):
+        radial_phase(phase)
+
+        @pl.when(phase == 0)
+        def _():
+            turn_weights(5, 9)
+
+        back(phase)
+
+        @pl.when(phase < 2)
+        def _():
+            def body(order, _):
+                term(phase, order)
+                return 0
+
+            lax.fori_loop(0, 3, body, 0)
+
+        return 0
+
+    lax.fori_loop(0, PHASES, one_phase, 0)
     for j in range(CH // TILE):
         cols = slice(j * TILE, (j + 1) * TILE)
         out[cols, :] = v[:, cols].T
 
-    for phase in range(PHASES):
-        for i in range(GROUP):
-
+    def end_phase(phase, _):
+        def body(i, _):
             @pl.when(g != i)
             def _():
                 in_copy(phase, i).wait_send()
                 out_copy(phase, i).wait_send()
 
-    for t in range(TERMS):
-        for part in range(len(PARTS)):
+            @pl.when(jnp.logical_and(has_far, phase < 2))
+            def _():
+                direct_copy(phase, i).wait_send()
+
+            return 0
+
+        return lax.fori_loop(0, GROUP, body, 0)
+
+    lax.fori_loop(0, PHASES, end_phase, 0)
+
+    def end_term(t, _):
+        for part in range(PARTS):
             near_copy(t, part).wait_send()
 
-    @pl.when(has_far)
-    def _():
-        for step in range(2):
-            for i in range(GROUP):
-                direct_copy(step, i).wait_send()
-        for t in range(TERMS):
-            if t % 3:
-                for part in range(len(PARTS)):
-                    for j in range(CH // FINE):
-                        far_copy(t, part, j).wait_send()
+            @pl.when(jnp.logical_and(has_far, t % 3 > 0))
+            def _():
+                far_copy(t, part).wait_send()
+
+        return 0
+
+    lax.fori_loop(0, TERMS, end_term, 0)
 
 
 def shards(
@@ -414,8 +449,8 @@
         scratch_shapes=[
             pltpu.VMEM((9, CH, CH), BF16),
             pltpu.VMEM((3, CH, ORDERS * CH), BF16),
-            pltpu.VMEM((TERMS, 3, COLS, CH), BF16),
-            pltpu.VMEM((2, GROUP, 2 * PART, HALF), BF16),
+            pltpu.VMEM((TERMS + 1, 3, COLS, CH), BF16),
+            pltpu.VMEM((PHASES, GROUP, 2 * PART, HALF), BF16),
             pltpu.VMEM((PHASES, GROUP, BLOCK, PART, TILE), jnp.int16),
             pltpu.VMEM((PHASES, GROUP, BLOCK, PART, TILE), jnp.int16),
             pltpu.VMEM((PHASES, GROUP, BLOCK, PART, TILE), jnp.int16),
@@ -423,7 +458,7 @@
             pltpu.VMEM((COLS, CH), F32),
             pltpu.VMEM((COLS, ORDERS * CH), F32),
             pltpu.VMEM((COLS, CH), F32),
-            pltpu.VMEM((COLS, CH), F32),
+            pltpu.VMEM((2 * TILE, HALF), F32),
             pltpu.VMEM((TILE, HALF), F32),
             pltpu.VMEM((TILE, HALF), F32),
             pltpu.VMEM((CH, COLS), F32),
@@ -441,10 +476,10 @@
             dma((PHASES, GROUP)),
             dma((PHASES, GROUP)),
             dma((PHASES, GROUP)),
-            dma((TERMS, len(PARTS))),
-            dma((TERMS, len(PARTS))),
-            dma((TERMS, len(PARTS), CH // FINE)),
-            dma((TERMS, len(PARTS), CH // FINE)),
+            dma((TERMS, PARTS)),
+            dma((TERMS, PARTS)),
+            dma((TERMS, PARTS)),
+            dma((TERMS, PARTS)),
             dma((2, GROUP)),
             dma((2, GROUP)),
         ],

time: 80.2 us -> 77.6 us (0.968)
  Pallas kernels: 77.6 us -> 75.1 us
    pallas_call x1, Pallas kernels: 77.6 us -> 75.1 us  [shards(): pl.pallas_call(kernel, out_shape=jax.ShapeDtypeStruct((CH, COLS), F32), i...]
where the time goes in v3:
time: 77.6 us; the launch traced here: 77.5 us
  Pallas kernels  75.1 us (97%)
  local copies, waits for them, and re-layouts  1.77 us (2%)
    pallas_call x1, Pallas kernels, shards(): pl.pallas_call(kernel, out_shape=jax.ShapeDtypeStruct((CH, COLS), F32), i...  75.1 us
    unnamed x1, local copies, waits for them, and re-layouts  1.77 us

profile of v3, /device:TPU:64, one launch (start us, length us, event | category | flops | bytes accessed | tf_op | source)
XLA Modules:
  0.0 77.5 jit_solution(2302335013839073413)
XLA Ops:
  0.7 75.1 %shard_map.82 = f32[768,128]{1,0:T(8,128)} custom-call(s32[1]{0:T(128)S(6)} %copy.11.counts, s32[6,3,1,6]{3,2,1,0:T(1,128)} %bitcast.14, f32[768,128]{1,0:T(8,128)} %bitcast.13, bf16[9,768,768]{2,1,0:T(8,128)(2,1)} %bitcast.11, f32[3,16]{1,0:T(4,128)} %radial_h.1, f32[1,768]{1,0:T(1,128)} %energy_h.1, f32[4,128]{1,0:T(4,128)} %bitcast.15, ...), custom_call_target="tpu_custom_call" | custom-call | tf_op jit(solution)/shard_map/pallas_call | solution.py:444
  75.7 1.8 %copy.12 = f32[1,768,1,128]{3,2,1,0:T(1,128)} copy(f32[1,768,1,128]{3,2,1,0:T(1,128)} %bitcast.12) | data formatting | bytes 786432

commit v4 on v3

--- a/solution.py
+++ b/solution.py
@@ -280,13 +280,21 @@
             im = turned[128 + i * PART : 128 + (i + 1) * PART]
             hout[phase, i, :PART] = re.astype(BF16)
             hout[phase, i, PART:] = im.astype(BF16)
+
+        @pl.when(jnp.logical_and(has_far, phase < 2))
+        def _():
+            def straight(i, _):
+                direct_copy(phase, i).start()
+                return 0
+
+            lax.fori_loop(0, GROUP, straight, 0)
+
+        for i in range(GROUP):
+            re = turned[i * PART : (i + 1) * PART]
+            im = turned[128 + i * PART : 128 + (i + 1) * PART]
             pack(re, im, qout.at[phase, i])
 
         def send(i, _):
-            @pl.when(jnp.logical_and(has_far, phase < 2))
-            def _():
-                direct_copy(phase, i).start()
-
             @pl.when(g != i)
             def _():
                 out_copy(phase, i).start()

time: 77.6 us -> 79.9 us (1.030)
  Pallas kernels: 75.1 us -> 77.3 us
    pallas_call x1, Pallas kernels: 75.1 us -> 77.3 us  [shards(): pl.pallas_call(kernel, out_shape=jax.ShapeDtypeStruct((CH, COLS), F32), i...]
where the time goes in v4:
time: 79.9 us; the launch traced here: 79.7 us
  Pallas kernels  77.3 us (97%)
  local copies, waits for them, and re-layouts  1.77 us (2%)
    pallas_call x1, Pallas kernels, shards(): pl.pallas_call(kernel, out_shape=jax.ShapeDtypeStruct((CH, COLS), F32), i...  77.3 us
    unnamed x1, local copies, waits for them, and re-layouts  1.77 us

profile of v4, /device:TPU:64, one launch (start us, length us, event | category | flops | bytes accessed | tf_op | source)
XLA Modules:
  0.0 79.7 jit_solution(2882085098512952142)
XLA Ops:
  0.7 77.3 %shard_map.82 = f32[768,128]{1,0:T(8,128)} custom-call(s32[1]{0:T(128)S(6)} %copy.11.counts, s32[6,3,1,6]{3,2,1,0:T(1,128)} %bitcast.14, f32[768,128]{1,0:T(8,128)} %bitcast.13, bf16[9,768,768]{2,1,0:T(8,128)(2,1)} %bitcast.11, f32[3,16]{1,0:T(4,128)} %radial_h.1, f32[1,768]{1,0:T(1,128)} %energy_h.1, f32[4,128]{1,0:T(4,128)} %bitcast.15, ...), custom_call_target="tpu_custom_call" | custom-call | tf_op jit(solution)/shard_map/pallas_call | solution.py:452
  78.0 1.8 %copy.12 = f32[1,768,1,128]{3,2,1,0:T(1,128)} copy(f32[1,768,1,128]{3,2,1,0:T(1,128)} %bitcast.12) | data formatting | bytes 786432
